TPU v7x, 512 devices: a whole 4x8x8 slice. The times are simulated.
512 devices in a mesh: seq: 64 (over z_lo, y, core), tp: 8 (over z_hi, x).
Axes of the slice: x: 4, y: 8, z: 8 (z_hi: 2, z_lo: 4; z = z_hi * 4 + z_lo), core: 2. Of those that a mesh axis runs over, the one named last changes fastest.
Arguments:
- queries: bfloat16 [512, 128, 128], P('seq', 'tp'), may hold values from -92 to 92
- prefix_keys: bfloat16 [32768, 8, 128], P('seq', 'tp'), may hold values from -5 to 5
- prefix_values: bfloat16 [32768, 8, 128], P('seq', 'tp'), may hold values from -12 to 12
- suffix_keys: bfloat16 [512, 256, 8, 128], P('seq', None, 'tp'), may hold values from -8 to 8
- suffix_values: bfloat16 [512, 256, 8, 128], P('seq', None, 'tp'), may hold values from -12 to 12
- self_keys: bfloat16 [512, 8, 128], P('seq', 'tp'), may hold values from -12 to 12
- self_values: bfloat16 [512, 8, 128], P('seq', 'tp'), may hold values from -12 to 12
- suffix_lengths: int32 [512], P('seq'), may hold values from 1 to 256, as said below
- out_weight: bfloat16 [16384, 16384], P('tp', 'seq'), may hold values from -0.046875 to 0.046875
Outputs:
- mixed: bfloat16 [512, 16384], P('tp', 'seq')
Inputs may be any that keep to these rules, and one draw needn't show every extreme that they name: `suffix_lengths`: at least one row has all 256 slots live and at least one has a single live slot.
All inputs are finite; a program needn't handle non-finite values.
Results may differ from a plain program's by a relative error of at most 0.025.
Values may be sent and summed in bfloat16 or wider, within the bound.
A program may use at most 128 MiB of HBM per device.

v0:
```python
import math

import jax
import jax.numpy as jnp
from jax import lax
from jax.sharding import PartitionSpec as P

EPS = 1e-06


def masked_scores(scores, live_mask):
    if live_mask is None:
        return scores
    return jnp.where(live_mask, scores, 0.0)


def softpick_terms(scores, live_mask, row_top, weighing):
    scores = masked_scores(scores, live_mask)
    shifted = jnp.exp(scores - row_top[..., None]) - jnp.exp(-row_top)[..., None]
    if live_mask is not None:
        shifted = jnp.where(live_mask, shifted, 0.0)
    weights = jnp.maximum(shifted, 0.0).astype(jnp.bfloat16)
    return (weighing(weights), jnp.sum(jnp.abs(shifted), axis=-1))


def absorb(running, scores, live_mask, weighing):
    row_top, numerator, denominator = running
    new_top = jnp.maximum(row_top, jnp.max(masked_scores(scores, live_mask), axis=-1))
    rescale = jnp.exp(row_top - new_top)
    part_num, part_den = softpick_terms(scores, live_mask, new_top, weighing)
    return (new_top, numerator * rescale[..., None] + part_num, denominator * rescale + part_den)


def finish(row_top, numerator, denominator):
    return (numerator / (denominator + EPS * jnp.exp(-row_top))[..., None]).astype(jnp.bfloat16)


def on_device(
    queries,
    prefix_keys,
    prefix_values,
    suffix_keys,
    suffix_values,
    self_keys,
    self_values,
    suffix_lengths,
    out_weight,
):
    own_rows, head_count, head_size = queries.shape
    kv_local = prefix_keys.shape[1]
    group_size = head_count // kv_local
    slot_count = suffix_keys.shape[1]
    inv_root = 1.0 / math.sqrt(head_size)
    own_query = queries.reshape(own_rows, kv_local, group_size, head_size)
    live_mask = (jnp.arange(slot_count, dtype=jnp.int32)[None, :] < suffix_lengths[:, None])[
        :, None, None, :
    ]
    suffix_scores = (
        jnp.einsum("rkgd,rskd->rkgs", own_query, suffix_keys, preferred_element_type=jnp.float32)
        * inv_root
    )
    self_scores = (
        jnp.einsum("rkgd,rkd->rkg", own_query, self_keys, preferred_element_type=jnp.float32)[
            ..., None
        ]
        * inv_root
    )

    def weigh_suffix(weights):
        return jnp.einsum(
            "rkgs,rskd->rkgd", weights, suffix_values, preferred_element_type=jnp.float32
        )

    def weigh_self(weights):
        return jnp.einsum(
            "rkgs,rksd->rkgd",
            weights,
            self_values[:, :, None, :],
            preferred_element_type=jnp.float32,
        )

    empty_row = jnp.zeros((own_rows, kv_local, group_size), jnp.float32)
    running = (
        empty_row,
        jnp.zeros((own_rows, kv_local, group_size, head_size), jnp.float32),
        empty_row,
    )
    running = absorb(running, suffix_scores, live_mask, weigh_suffix)
    running = absorb(running, self_scores, None, weigh_self)
    key_block = lax.all_gather(prefix_keys, "seq", axis=0, tiled=True)
    value_block = lax.all_gather(prefix_values, "seq", axis=0, tiled=True)
    scores = (
        jnp.einsum("rkgd,pkd->rkgp", own_query, key_block, preferred_element_type=jnp.float32)
        * inv_root
    )

    def weigh_block(weights):
        return jnp.einsum(
            "rkgp,pkd->rkgd", weights, value_block, preferred_element_type=jnp.float32
        )

    row_top, numerator, denominator = absorb(running, scores, None, weigh_block)
    own_attention = finish(row_top, numerator, denominator).reshape(
        own_rows, head_count * head_size
    )
    attention = lax.all_gather(own_attention, "seq", axis=0, tiled=True)
    return lax.psum_scatter(
        jnp.dot(attention, out_weight, preferred_element_type=jnp.float32).astype(jnp.bfloat16),
        "tp",
        scatter_dimension=0,
        tiled=True,
    )


def solution(mesh):
    return jax.shard_map(
        on_device,
        mesh=mesh,
        in_specs=(
            P("seq", "tp", None),
            P("seq", "tp", None),
            P("seq", "tp", None),
            P("seq", None, "tp", None),
            P("seq", None, "tp", None),
            P("seq", "tp", None),
            P("seq", "tp", None),
            P("seq"),
            P("tp", "seq"),
        ),
        out_specs=P("tp", "seq"),
        check_vma=False,
    )
```

profile of v0, /device:TPU:1, one launch (start us, length us, event | category | flops | bytes accessed | tf_op | source)
XLA Modules:
  0.0 488.4 jit_solution(18115628801041145744)
XLA Ops:
  6.5 0.0 copy-start
  6.5 0.0 all-gather.4.cloned.1.call-start
  6.5 0.7 all-gather.4.cloned.1.call-update
  7.3 0.0 all-gather.6.cloned.1.call-start
  7.3 0.7 all-gather.6.cloned.1.call-update
  8.0 0.0 all-gather.8.cloned.1.call-start
  8.1 0.7 iota_compare_fusion
  8.8 0.7 bitcast_convert_fusion
  9.5 0.9 fusion.29
  10.3 1.4 fusion.36
  11.7 129.3 %all-gather.4.cloned.1.call-done = bf16[32768,1,128]{2,0,1:T(8,128)(2,1)} async-done(((bf16[512,1,128]{2,0,1:T(8,128)(2,1)}), bf16[32768,1,128]{2,0,1:T(8,128)(2,1)}) %all-gather.4.cloned.1.call-update) | async-done | bytes 8388624 | tf_op jit(solution)/shard_map/all_gather | solution.py:90
  141.0 11.5 %fusion.37 = (f32[8,16]{1,0:T(8,128)S(1)}, f32[8,1,16,32768]{3,2,0,1:T(8,128)}) fusion(bf16[8,16,128]{2,1,0:T(8,128)(2,1)} %param.9, bf16[32768,1,128]{2,0,1:T(8,128)(2,1)} %all-gather.4.cloned.1.call-done), kind=kOutput, calls=%fused_computation.54 | convolution fusion | flops 1082130304 | bytes 25199104 | tf_op jit(solution)/shard_map/rkgd,pkd->rkgp/dot_general | solution.py:93
  152.5 0.2 abs_reduce_fusion.1
  152.7 9.3 %abs_reduce_fusion = f32[8,16]{1,0:T(8,128)S(1)} fusion(f32[8,1,16,32768]{3,2,0,1:T(8,128)} %get-tuple-element.19, f32[8,16]{1,0:T(8,128)S(1)} %negate_exponential_fusion, f32[8,16]{1,0:T(8,128)S(1)} %get-tuple-element.14), kind=kLoop, calls=%fused_computation.2 | loop fusion | flops 16777088 | bytes 16778752 | tf_op jit(solution)/shard_map/reduce_sum | solution.py:23
  162.0 0.0 copy-start.1
  162.1 103.6 %all-gather.6.cloned.1.call-done = bf16[32768,1,128]{2,0,1:T(8,128)(2,1)} async-done(((bf16[512,1,128]{2,0,1:T(8,128)(2,1)}), bf16[32768,1,128]{2,0,1:T(8,128)(2,1)}) %all-gather.6.cloned.1.call-update) | async-done | bytes 8388624 | tf_op jit(solution)/shard_map/all_gather | solution.py:91
  265.7 11.4 %fusion.10 = f32[8,1,16,128]{3,2,0,1:T(8,128)S(1)} fusion(bf16[32768,1,128]{2,0,1:T(8,128)(2,1)} %all-gather.6.cloned.1.call-done, f32[8,1,16,32768]{3,2,0,1:T(8,128)} %get-tuple-element.19, f32[8,16]{1,0:T(8,128)S(1)} %negate_exponential_fusion, f32[8,16]{1,0:T(8,128)S(1)} %get-tuple-element.14), kind=kOutput, calls=%fused_computation.15 | convolution fusion | flops 1090519040 | bytes 25232384 | tf_op jit(solution)/shard_map/rkgp,pkd->rkgd/dot_general | solution.py:98
  277.1 0.0 copy-done.1
  277.1 0.3 fusion.22
  277.4 0.6 copy.16
  278.0 0.0 all-gather.8.cloned.1.call-update
  278.0 0.0 reduce-scatter.2.cloned.1.call-start
  278.1 115.6 %all-gather.8.cloned.1.call-done = bf16[512,2048]{1,0:T(8,128)(2,1)} async-done(((bf16[8,2048]{1,0:T(8,128)(2,1)}), bf16[512,2048]{1,0:T(8,128)(2,1)}) %all-gather.8.cloned.1.call-update) | async-done | bytes 2097168 | tf_op jit(solution)/shard_map/all_gather | solution.py:106
  393.7 0.0 copy-done
  393.7 3.0 convolution_convert_fusion
  396.7 0.0 reduce-scatter.2.cloned.1.call-update
  396.8 85.1 %reduce-scatter.2.cloned.1.call-done = bf16[64,256]{1,0:T(8,128)(2,1)} async-done(((bf16[512,256]{1,0:T(8,128)(2,1)}), bf16[64,256]{1,0:T(8,128)(2,1)}) %reduce-scatter.2.cloned.1.call-update) | async-done | bytes 32784 | tf_op jit(solution)/shard_map/reduce_scatter | solution.py:107
  (3 shorter events, 0.0 us)
Async XLA Ops:
  6.5 387.2 %copy-start = (bf16[2048,256]{1,0:T(8,128)(2,1)S(1)}, bf16[2048,256]{1,0:T(8,128)(2,1)}, u32[]{:S(2)}) copy-start(bf16[2048,256]{1,0:T(8,128)(2,1)} %param.17) | copy-start | bytes 3145732
  6.5 134.5 %all-gather.4.cloned.1.call-start = ((), (), s32[]{:S(2)}) async-start(), calls=%async_computation.1 | async-start | bytes 8519680 | tf_op jit(solution)/shard_map/all_gather | solution.py:90
  7.3 258.4 %all-gather.6.cloned.1.call-start = ((), (), s32[]{:S(2)}) async-start(), calls=%async_computation.2 | async-start | bytes 8519680 | tf_op jit(solution)/shard_map/all_gather | solution.py:91
  8.0 385.7 %all-gather.8.cloned.1.call-start = ((), (), s32[]{:S(2)}) async-start(), calls=%async_computation.3 | async-start | bytes 2129920 | tf_op jit(solution)/shard_map/all_gather | solution.py:106
  162.0 115.1 %copy-start.1 = (bf16[8,256,1,128]{3,1,2,0:T(8,128)(2,1)S(1)}, bf16[8,256,1,128]{3,1,2,0:T(8,128)(2,1)}, u32[]{:S(2)}) copy-start(bf16[8,256,1,128]{3,1,2,0:T(8,128)(2,1)} %param.13) | copy-start | bytes 1572868
  278.0 203.8 %reduce-scatter.2.cloned.1.call-start = ((), (), s32[]{:S(2)}) async-start(), calls=%async_computation.4 | async-start | bytes 294912 | tf_op jit(solution)/shard_map/reduce_scatter | solution.py:107
Sparse Core Ops, SparseCore 0:
  9.5 131.4 all-gather.3
  143.1 122.4 all-gather.5
  278.2 115.5 all-gather.7
  398.0 83.8 reduce-scatter.1
where the time goes:
time: 490 us; the launch traced here: 488 us
  waiting for transfers between devices  435 us (89%)
  matrix products  28.4 us (6%)
  between operations  13.2 us (3%)
  other arithmetic  11 us (2%)
    all_gather x1, waiting for transfers between devices, on_device(): key_block = lax.all_gather(prefix_keys, 'seq', axis=0, tiled=True)  129 us
    all_gather x1, waiting for transfers between devices, on_device(): attention = lax.all_gather(own_attention, 'seq', axis=0, tiled=True)  116 us
    all_gather x1, waiting for transfers between devices, on_device(): value_block = lax.all_gather(prefix_values, 'seq', axis=0, tiled=True)  104 us
    reduce_scatter x1, waiting for transfers between devices, on_device(): lax.psum_scatter(jnp.dot(attention, out_weight, preferred_element_type=jn...  85.1 us
    dot_general x1, matrix products, on_device(): jnp.einsum('rkgd,pkd->rkgp', own_query, key_block, preferred_element_type...  11.5 us
    dot_general x1, matrix products, weigh_block(): jnp.einsum('rkgp,pkd->rkgd', weights, value_block, preferred_element_type...  11.4 us
  transfers between devices with their start and end apart: 4, of which 4 were waited for; matrix products, arithmetic and copies ran while one was open for 5% of the time, Pallas kernels for 0%

commit v1 on v0

v1 whole, which is shorter than its diff:
```python
import functools
import math

import jax
import jax.numpy as jnp
from jax import lax
from jax.experimental import pallas as pl
from jax.experimental.pallas import tpu as pltpu
from jax.sharding import PartitionSpec as P

EPS = 1e-06
MESH = pl.DeviceIdType.MESH
F32 = jnp.float32
BF16 = jnp.bfloat16

NZ, NY, NX, NZH = 4, 8, 4, 2
QROWS = 128
KEYS = 512
TILE = 256


def coordinates():
    s = lax.axis_index("seq")
    t = lax.axis_index("tp")
    return s // 16, lax.rem(s // 2, NY), lax.rem(s, 2), t // NX, lax.rem(t, NX)


def device(z, y, c, zh, x):
    return ((z * NY + y) * 2 + c, zh * NX + x)


def kernel(
    q_hbm, pk_hbm, pv_hbm, sk_hbm, sv_hbm, w_hbm, selfk_ref, selfv_ref, len_ref,
    out_ref,
    qbuf, kbuf, vbuf, skbuf, svbuf, selfk, selfv, wbuf,
    num, top, den, pn_out, ps_out, pn_in, ps_in, att, land, rows_all, prod, pieces,
    local_sem, send_sem, recv_sem,
):
    z, y, c, zh, x = coordinates()
    z_near = z + 1 - 2 * lax.rem(z, 2)
    y_near = y + 1 - 2 * lax.rem(y, 2)
    other = 1 - c
    scale = math.log2(math.e) / math.sqrt(128)

    local = [
        pltpu.make_async_copy(src, dst, local_sem.at[i])
        for i, (src, dst) in enumerate(
            [
                (q_hbm, qbuf.at[pl.ds(0, QROWS)]),
                (pk_hbm, kbuf.at[0, pl.ds(0, KEYS)]),
                (pv_hbm, vbuf.at[0, pl.ds(0, KEYS)]),
                (sk_hbm, skbuf),
                (sv_hbm, svbuf),
                (w_hbm, wbuf.at[0]),
            ]
        )
    ]
    for copy in local:
        copy.start()

    dev_core = device(z, y, other, zh, x)
    dev_ynear = device(z, y_near, c, zh, x)
    dev_znear = device(z_near, y, c, zh, x)

    def coset(r, sign):
        if sign > 0:
            zz = lax.rem(z + 2 * (r // 4), NZ)
            yy = lax.rem(y + 2 * lax.rem(r, 4), NY)
        else:
            zz = lax.rem(z + NZ - 2 * (r // 4), NZ)
            yy = lax.rem(y + NY - 2 * lax.rem(r, 4), NY)
        return device(zz, yy, c, zh, x)

    def line(r):
        return device(lax.rem(z + NZ - r, NZ), y, c, zh, x)

    dev_right = device(z, lax.rem(y + 1, NY), c, zh, x)
    dev_left = device(z, lax.rem(y + NY - 1, NY), c, zh, x)

    def owner(r):
        return device(
            z, y, lax.rem(c + lax.rem(r, 2), 2), lax.rem(zh + r // 8, NZH), lax.rem(x + lax.rem(r // 2, 4), NX)
        )

    partners = [dev_znear, dev_right, dev_left]
    partners += [coset(r, 1) for r in range(1, 8)]
    partners += [line(r) for r in range(1, NZ)]
    partners += [owner(r) for r in range(1, 16)]
    barrier = pltpu.get_barrier_semaphore()
    for partner in partners:
        pl.semaphore_signal(barrier, inc=1, device_id=partner, device_id_type=MESH)
    pl.semaphore_wait(barrier, len(partners))

    slots = iter(range(1000))

    def remote(src, dst, to, slot=None):
        slot = next(slots) if slot is None else slot
        return pltpu.make_async_remote_copy(
            src_ref=src, dst_ref=dst, send_sem=send_sem.at[slot], recv_sem=recv_sem.at[slot],
            device_id=to, device_id_type=MESH,
        )

    started = []

    def go(copy):
        copy.start()
        started.append(copy)
        return copy

    local[0].wait()
    q_copies = [
        go(remote(qbuf.at[pl.ds(0, QROWS)], qbuf.at[pl.ds(r * QROWS, QROWS)], coset(r, 1)))
        for r in range(1, 8)
    ]
    low, high = pl.ds(0, KEYS), pl.ds(KEYS, KEYS)
    local[1].wait()
    local[2].wait()
    k_core = [None] * 4
    v_core = [None] * 4
    k_y = go(remote(kbuf.at[0, low], kbuf.at[1, low], dev_ynear))
    v_z = go(remote(vbuf.at[0, low], vbuf.at[2, low], dev_znear))
    v_y = go(remote(vbuf.at[0, low], vbuf.at[1, low], dev_ynear))
    k_z = go(remote(kbuf.at[0, low], kbuf.at[2, low], dev_znear))
    k_core[0] = go(remote(kbuf.at[0, low], kbuf.at[0, high], dev_core))
    v_core[0] = go(remote(vbuf.at[0, low], vbuf.at[0, high], dev_core))

    for copy in local[3:5]:
        copy.wait()
    selfk[...] = selfk_ref[...].astype(F32)
    selfv[...] = selfv_ref[...].astype(F32)
    num[...] = jnp.zeros_like(num)
    top[...] = jnp.zeros_like(top)
    den[...] = jnp.zeros_like(den)

    def one_row(r, carry):
        rows = pl.ds(pl.multiple_of(r * 16, 16), 16)
        q = qbuf[rows, :]
        s = lax.dot_general(q, skbuf[r], (((1,), (1,)), ((), ())), preferred_element_type=F32) * scale
        live = lax.broadcasted_iota(jnp.int32, s.shape, 1) < len_ref[r]
        s = jnp.where(live, s, 0.0)
        s_self = jnp.sum(q.astype(F32) * selfk[pl.ds(r, 1), :], axis=1, keepdims=True) * scale
        m = jnp.maximum(jnp.maximum(jnp.max(s, axis=1, keepdims=True), s_self), 0.0)
        base = jnp.exp2(-m)
        shifted = jnp.where(live, jnp.exp2(s - m) - base, 0.0)
        shifted_self = jnp.exp2(s_self - m) - base
        weights = jnp.maximum(shifted, 0.0).astype(BF16)
        weight_self = jnp.maximum(shifted_self, 0.0).astype(BF16).astype(F32)
        total = jnp.dot(weights, svbuf[r], preferred_element_type=F32)
        num[rows, :] = total + weight_self * selfv[pl.ds(r, 1), :]
        size = jnp.abs(shifted)
        size = size[:, :128] + size[:, 128:]
        lane = lax.broadcasted_iota(jnp.int32, size.shape, 1)
        den[rows, :] = size + jnp.where(lane == 0, jnp.abs(shifted_self), 0.0)
        top[rows, :] = jnp.broadcast_to(m, size.shape)
        return carry

    lax.fori_loop(0, 8, one_row, 0)

    def absorb(g, i):
        rows = pl.ds(pl.multiple_of(i * TILE, TILE), TILE)
        s = lax.dot_general(
            qbuf[rows, :], kbuf[g], (((1,), (1,)), ((), ())), preferred_element_type=F32
        ) * scale
        old = top[rows, :]
        new = jnp.maximum(old, jnp.max(s, axis=1, keepdims=True))
        base = jnp.exp2(-new)
        rescale = jnp.exp2(old - new)
        size = den[rows, :] * rescale
        weights = []
        for j in range(2 * KEYS // 128):
            shifted = jnp.exp2(s[:, j * 128 : (j + 1) * 128] - new) - base
            weights.append(jnp.maximum(shifted, 0.0).astype(BF16))
            size = size + jnp.abs(shifted)
        weights = jnp.concatenate(weights, axis=1)
        total = num[rows, :] * rescale + jnp.dot(weights, vbuf[g], preferred_element_type=F32)
        return rows, new, size, total

    def stage(g):
        def tile(i, carry):
            rows, new, size, total = absorb(g, i)
            top[rows, :] = new
            den[rows, :] = size
            num[rows, :] = total
            return carry

        lax.fori_loop(0, 8 * QROWS // TILE, tile, 0)

    k_core[0].wait_recv()
    v_core[0].wait_recv()
    for copy in q_copies:
        copy.wait_recv()
    stage(0)
    k_y.wait_recv()
    k_d = go(remote(kbuf.at[1, low], kbuf.at[3, low], dev_znear))
    v_z.wait_recv()
    v_d = go(remote(vbuf.at[2, low], vbuf.at[3, low], dev_ynear))
    v_y.wait_recv()
    k_core[1] = go(remote(kbuf.at[1, low], kbuf.at[1, high], dev_core))
    v_core[1] = go(remote(vbuf.at[1, low], vbuf.at[1, high], dev_core))
    k_z.wait_recv()
    k_core[2] = go(remote(kbuf.at[2, low], kbuf.at[2, high], dev_core))
    v_core[2] = go(remote(vbuf.at[2, low], vbuf.at[2, high], dev_core))
    k_core[1].wait_recv()
    v_core[1].wait_recv()
    stage(1)
    k_core[2].wait_recv()
    v_core[2].wait_recv()
    stage(2)
    k_d.wait_recv()
    k_core[3] = go(remote(kbuf.at[3, low], kbuf.at[3, high], dev_core))
    v_d.wait_recv()
    v_core[3] = go(remote(vbuf.at[3, low], vbuf.at[3, high], dev_core))
    local[5].wait()
    w_copy = go(remote(wbuf.at[0], wbuf.at[1], dev_core))
    k_core[3].wait_recv()
    v_core[3].wait_recv()

    part_slots = [(next(slots), next(slots)) for _ in range(7)]
    first_slot = part_slots[0][0]

    def stat_rows(new, size):
        lane = lax.broadcasted_iota(jnp.int32, new.shape, 1)
        both = jnp.where(lane == 0, new, jnp.where(lane == 1, jnp.sum(size, axis=1, keepdims=True), 0.0))
        return both.T[0:8, :]

    def part_copies(r):
        rows = pl.ds(pl.multiple_of(r * QROWS, QROWS), QROWS)
        stat = pl.ds(pl.multiple_of(r * 8, 8), 8)
        to = coset(r, -1)
        slot = first_slot + 2 * (r - 1)
        return (
            remote(pn_out.at[rows], pn_in.at[rows], to, slot),
            remote(ps_out.at[stat], ps_in.at[stat], to, slot + 1),
        )

    def last(i):
        rows, new, size, total = absorb(3, i)
        pn_out[rows, :] = total.astype(BF16)
        for half in range(2):
            part = slice(half * QROWS, (half + 1) * QROWS)
            r = i * 2 + half
            ps_out[pl.ds(pl.multiple_of(r * 8, 8), 8), :] = stat_rows(new[part], size[part])
        return total

    def last_tile(step, carry):
        i = 3 - step
        last(i)
        for half in range(2):
            for copy in part_copies(i * 2 + half):
                copy.start()
        return carry

    lax.fori_loop(0, 3, last_tile, 0)
    total = last(0)
    for copy in part_copies(1):
        copy.start()
    num[pl.ds(0, QROWS), :] = total[:QROWS]

    for r in range(1, 8):
        for copy in part_copies(r):
            copy.wait_recv()
            started.append(copy)
    tops = jnp.concatenate([ps_out[0:1, :]] + [ps_in[r * 8 : r * 8 + 1, :] for r in range(1, 8)], axis=0)
    dens = jnp.concatenate([ps_out[1:2, :]] + [ps_in[r * 8 + 1 : r * 8 + 2, :] for r in range(1, 8)], axis=0)
    new = jnp.max(tops, axis=0, keepdims=True)
    rescale = jnp.exp2(tops - new)
    bottom = jnp.sum(rescale * dens, axis=0, keepdims=True) + EPS * jnp.exp2(-new)
    factor = rescale / bottom
    factor = jnp.concatenate([factor, jnp.zeros((120, 128), F32)], axis=0).T
    total = num[pl.ds(0, QROWS), :] * factor[:, 0:1]
    for r in range(1, 8):
        total = total + pn_in[pl.ds(r * QROWS, QROWS), :].astype(F32) * factor[:, r : r + 1]
    att[...] = total
    by_head = [att[pl.ds(h, 8, stride=16), :] for h in range(16)]
    own = z * NY + y
    land[own] = jnp.concatenate(by_head, axis=0).astype(BF16)

    z_copies = [None] + [go(remote(land.at[own], land.at[own], line(r))) for r in range(1, NZ)]
    arrived = {}
    for k in range(4):
        for r in range(NZ):
            zz = lax.rem(z + r, NZ)
            if k == 0 and r > 0:
                z_copies[r].wait_recv()
            for way in range(2):
                if k > 0:
                    arrived[way, k - 1, r].wait_recv()
                if k == 3 and (r < 2) != (way == 0):
                    continue
                yy = lax.rem(y + NY - k, NY) if way == 0 else lax.rem(y + k, NY)
                block = land.at[zz * NY + yy]
                arrived[way, k, r] = go(remote(block, block, dev_right if way == 0 else dev_left))
    for r in range(NZ):
        arrived[0 if r < 2 else 1, 3, r].wait_recv()

    w_copy.wait_recv()
    for j in range(8):
        pair = land[:, j * 16 : (j + 1) * 16, :].astype(F32).reshape(32, 2, 8, 128)
        for half in range(2):
            h = 2 * j + half
            rows_all[:, h * 128 : (h + 1) * 128] = pair[:, half].reshape(256, 128).astype(BF16)
    prod[0] = jnp.dot(rows_all[...], wbuf[0], preferred_element_type=F32).astype(BF16)
    prod[1] = jnp.dot(rows_all[...], wbuf[1], preferred_element_type=F32).astype(BF16)

    def piece(r):
        t = lax.rem(zh + r // 8, NZH) * NX + lax.rem(x + lax.rem(r // 2, 4), NX)
        return prod.at[r % 2, pl.ds(pl.multiple_of(t * 32, 32), 32)]

    out_copies = [go(remote(piece(r), pieces.at[r], owner(r))) for r in range(1, 16)]
    own_rows = pl.ds(pl.multiple_of((zh * NX + x) * 32, 32), 32)
    sums = [prod[0, own_rows, :].astype(F32), None]
    for r in range(1, 16):
        out_copies[r - 1].wait_recv()
        term = pieces[r].astype(F32)
        sums[r % 2] = term if sums[r % 2] is None else sums[r % 2] + term
    first = jnp.where(c == 0, sums[0], sums[1]).reshape(4, 1, 8, 256)
    second = jnp.where(c == 0, sums[1], sums[0]).reshape(4, 1, 8, 256)
    out_ref[...] = jnp.concatenate([first, second], axis=1).reshape(64, 256).astype(BF16)

    for copy in started:
        copy.wait_send()


def on_device(q, pk, pv, sk, sv, selfk, selfv, lengths, w):
    hbm = pl.BlockSpec(memory_space=pltpu.HBM)
    vmem = pltpu.VMEM
    return pl.pallas_call(
        kernel,
        out_shape=jax.ShapeDtypeStruct((64, 256), BF16),
        in_specs=[hbm] * 6 + [pl.BlockSpec(memory_space=vmem)] * 2 + [pl.BlockSpec(memory_space=pltpu.SMEM)],
        out_specs=pl.BlockSpec(memory_space=vmem),
        scratch_shapes=[
            vmem((8 * QROWS, 128), BF16),
            vmem((4, 2 * KEYS, 128), BF16),
            vmem((4, 2 * KEYS, 128), BF16),
            vmem((8, 256, 128), BF16),
            vmem((8, 256, 128), BF16),
            vmem((8, 128), F32),
            vmem((8, 128), F32),
            vmem((2, 2048, 256), BF16),
            vmem((8 * QROWS, 128), F32),
            vmem((8 * QROWS, 128), F32),
            vmem((8 * QROWS, 128), F32),
            vmem((8 * QROWS, 128), BF16),
            vmem((64, 128), F32),
            vmem((8 * QROWS, 128), BF16),
            vmem((64, 128), F32),
            vmem((QROWS, 128), F32),
            vmem((32, QROWS, 128), BF16),
            vmem((256, 2048), BF16),
            vmem((2, 256, 256), BF16),
            vmem((16, 32, 256), BF16),
            pltpu.SemaphoreType.DMA((6,)),
            pltpu.SemaphoreType.DMA((96,)),
            pltpu.SemaphoreType.DMA((96,)),
        ],
        compiler_params=pltpu.CompilerParams(
            collective_id=0, has_side_effects=True, vmem_limit_bytes=48 << 20
        ),
        name="attend_project",
    )(
        q.reshape(QROWS, 128), pk.reshape(KEYS, 128), pv.reshape(KEYS, 128),
        sk.reshape(8, 256, 128), sv.reshape(8, 256, 128), w, selfk.reshape(8, 128), selfv.reshape(8, 128), lengths,
    )


def solution(mesh):
    return jax.shard_map(
        on_device,
        mesh=mesh,
        in_specs=(
            P("seq", "tp", None),
            P("seq", "tp", None),
            P("seq", "tp", None),
            P("seq", None, "tp", None),
            P("seq", None, "tp", None),
            P("seq", "tp", None),
            P("seq", "tp", None),
            P("seq"),
            P("tp", "seq"),
        ),
        out_specs=P("tp", "seq"),
        check_vma=False,
    )
```

time: 490 us -> 84.6 us (0.17)
  waiting for transfers between devices: 435 us -> 0 us
  Pallas kernels: 0 us -> 77 us
  matrix products: 28.4 us -> 0 us
  between operations: 13.2 us -> 0.02 us
  other arithmetic: 11 us -> 0 us
  local copies, waits for them, and re-layouts: 0.64 us -> 7.18 us
    all_gather x3 -> x0, waiting for transfers between devices: 349 us -> none  [the longest x1 129 us: on_device(): key_block = lax.all_gather(prefix_keys, 'seq', axis=0, tiled=True)]
    reduce_scatter x1 -> x0, waiting for transfers between devices: 85.1 us -> none  [on_device(): lax.psum_scatter(jnp.dot(attention, out_weight, preferred_element_type=jn...]
    pallas_call x0 -> x1, Pallas kernels: none -> 77 us  [on_device(): pl.pallas_call(kernel, out_shape=jax.ShapeDtypeStruct((64, 256), BF16), i...]
    dot_general x6 -> x0, matrix products: 28.4 us -> none  [the longest x1 11.5 us: on_device(): jnp.einsum('rkgd,pkd->rkgp', own_query, key_block, preferred_element_type...]
    reduce_sum x2 -> x0, other arithmetic: 9.54 us -> none  [softpick_terms(): return (weighing(weights), jnp.sum(jnp.abs(shifted), axis=-1))]
    unnamed x5 -> x19, local copies, waits for them, and re-layouts: 0.64 us -> 7.18 us
  transfers between devices with their start and end apart: 4 -> 0, of which waited for: 4 -> 0; matrix products, arithmetic and copies ran while one was open for 5% -> 0% of each run, Pallas kernels for 0% -> 0%
where the time goes in v1:
time: 84.6 us; the launch traced here: 84.2 us
  Pallas kernels  77 us (91%)
  local copies, waits for them, and re-layouts  7.18 us (8%)
    pallas_call x1, Pallas kernels, on_device(): pl.pallas_call(kernel, out_shape=jax.ShapeDtypeStruct((64, 256), BF16), i...  77 us
    unnamed x19, local copies, waits for them, and re-layouts  7.18 us

profile of v1, /device:TPU:1, one launch (start us, length us, event | category | flops | bytes accessed | tf_op | source)
XLA Modules:
  0.0 84.2 jit_solution(6052734312740528442)
XLA Ops:
  0.0 0.0 copy-start.7
  0.0 0.0 copy-start.6
  0.0 0.0 copy-start.8
  0.0 0.7 copy-done.7
  0.7 0.0 copy-done.6
  0.7 0.0 copy-done.8
  0.7 0.0 copy-start
  0.7 1.2 %copy-done = bf16[2048,256]{1,0:T(8,128)(2,1)S(1)} copy-done((bf16[2048,256]{1,0:T(8,128)(2,1)S(1)}, bf16[2048,256]{1,0:T(8,128)(2,1)}, u32[]{:S(2)}) %copy-start) | copy-done | bytes 1048600
  1.9 0.0 copy-start.1
  1.9 1.0 %copy-done.1 = bf16[8,256,1,128]{3,1,2,0:T(8,128)(2,1)S(1)} copy-done((bf16[8,256,1,128]{3,1,2,0:T(8,128)(2,1)S(1)}, bf16[8,256,1,128]{3,1,2,0:T(8,128)(2,1)}, u32[]{:S(2)}) %copy-start.1) | copy-done | bytes 524312
  3.0 0.0 copy-start.2
  3.0 1.0 %copy-done.2 = bf16[8,256,1,128]{3,1,2,0:T(8,128)(2,1)S(1)} copy-done((bf16[8,256,1,128]{3,1,2,0:T(8,128)(2,1)S(1)}, bf16[8,256,1,128]{3,1,2,0:T(8,128)(2,1)}, u32[]{:S(2)}) %copy-start.2) | copy-done | bytes 524312
  4.0 0.0 copy-start.3
  4.0 0.9 %copy-done.3 = bf16[512,1,128]{2,0,1:T(8,128)(2,1)S(1)} copy-done((bf16[512,1,128]{2,0,1:T(8,128)(2,1)S(1)}, bf16[512,1,128]{2,0,1:T(8,128)(2,1)}, u32[]{:S(2)}) %copy-start.3) | copy-done | bytes 131096
  4.9 0.0 copy-start.4
  4.9 0.9 %copy-done.4 = bf16[512,1,128]{2,0,1:T(8,128)(2,1)S(1)} copy-done((bf16[512,1,128]{2,0,1:T(8,128)(2,1)S(1)}, bf16[512,1,128]{2,0,1:T(8,128)(2,1)}, u32[]{:S(2)}) %copy-start.4) | copy-done | bytes 131096
  5.8 0.0 copy-start.5
  5.8 0.8 copy-done.5
  6.6 77.0 %attend_project.1 = bf16[64,256]{1,0:T(8,128)(2,1)S(1)} custom-call(bf16[128,128]{1,0:T(8,128)(2,1)S(1)} %bitcast.11, bf16[512,128]{1,0:T(8,128)(2,1)S(1)} %bitcast.9, bf16[512,128]{1,0:T(8,128)(2,1)S(1)} %bitcast.10, bf16[8,256,128]{2,1,0:T(8,128)(2,1)S(1)} %bitcast.7, bf16[8,256,128]{2,1,0:T(8,128)(2,1)S(1)} %bitcast.8, bf16[2048,256]{1,0:T(8,128)(2,1)S(1)} %copy-done, ...), custom_call_target="tpu_custom_call" | custom-call | tf_op jit(solution)/shard_map/attend_project/pallas_call | solution.py:327
  83.6 0.6 copy.11
Async XLA Ops:
  0.0 0.7 copy-start.7
  0.0 0.7 copy-start.6
  0.0 0.7 copy-start.8
  0.7 1.2 %copy-start = (bf16[2048,256]{1,0:T(8,128)(2,1)S(1)}, bf16[2048,256]{1,0:T(8,128)(2,1)}, u32[]{:S(2)}) copy-start(bf16[2048,256]{1,0:T(8,128)(2,1)} %w_hbm.1) | copy-start | bytes 3145732
  1.9 1.0 %copy-start.1 = (bf16[8,256,1,128]{3,1,2,0:T(8,128)(2,1)S(1)}, bf16[8,256,1,128]{3,1,2,0:T(8,128)(2,1)}, u32[]{:S(2)}) copy-start(bf16[8,256,1,128]{3,1,2,0:T(8,128)(2,1)} %param.12) | copy-start | bytes 1572868
  3.0 1.0 %copy-start.2 = (bf16[8,256,1,128]{3,1,2,0:T(8,128)(2,1)S(1)}, bf16[8,256,1,128]{3,1,2,0:T(8,128)(2,1)}, u32[]{:S(2)}) copy-start(bf16[8,256,1,128]{3,1,2,0:T(8,128)(2,1)} %param.13) | copy-start | bytes 1572868
  4.0 0.9 %copy-start.3 = (bf16[512,1,128]{2,0,1:T(8,128)(2,1)S(1)}, bf16[512,1,128]{2,0,1:T(8,128)(2,1)}, u32[]{:S(2)}) copy-start(bf16[512,1,128]{2,0,1:T(8,128)(2,1)} %param.10) | copy-start | bytes 393220
  4.9 0.9 %copy-start.4 = (bf16[512,1,128]{2,0,1:T(8,128)(2,1)S(1)}, bf16[512,1,128]{2,0,1:T(8,128)(2,1)}, u32[]{:S(2)}) copy-start(bf16[512,1,128]{2,0,1:T(8,128)(2,1)} %param.11) | copy-start | bytes 393220
  5.8 0.8 copy-start.5

commit v2 on v1

--- a/solution.py
+++ b/solution.py
@@ -34,11 +34,10 @@
     out_ref,
     qbuf, kbuf, vbuf, skbuf, svbuf, selfk, selfv, wbuf,
     num, top, den, pn_out, ps_out, pn_in, ps_in, att, land, rows_all, prod, pieces,
-    local_sem, send_sem, recv_sem,
+    local_sem, send_sem, recv_sem, met,
 ):
     z, y, c, zh, x = coordinates()
     z_near = z + 1 - 2 * lax.rem(z, 2)
-    y_near = y + 1 - 2 * lax.rem(y, 2)
     other = 1 - c
     scale = math.log2(math.e) / math.sqrt(128)
 
@@ -59,7 +58,6 @@
         copy.start()
 
     dev_core = device(z, y, other, zh, x)
-    dev_ynear = device(z, y_near, c, zh, x)
     dev_znear = device(z_near, y, c, zh, x)
 
     def coset(r, sign):
@@ -82,10 +80,10 @@
             z, y, lax.rem(c + lax.rem(r, 2), 2), lax.rem(zh + r // 8, NZH), lax.rem(x + lax.rem(r // 2, 4), NX)
         )
 
-    partners = [dev_znear, dev_right, dev_left]
+    steps = [owner(1), owner(2), owner(6), owner(8)]
+    partners = [dev_right, dev_left] + steps
     partners += [coset(r, 1) for r in range(1, 8)]
     partners += [line(r) for r in range(1, NZ)]
-    partners += [owner(r) for r in range(1, 16)]
     barrier = pltpu.get_barrier_semaphore()
     for partner in partners:
         pl.semaphore_signal(barrier, inc=1, device_id=partner, device_id_type=MESH)
@@ -107,22 +105,29 @@
         started.append(copy)
         return copy
 
+    def meet(i):
+        for to in steps:
+            pl.semaphore_signal(met.at[i], inc=1, device_id=to, device_id_type=MESH)
+
     local[0].wait()
     q_copies = [
         go(remote(qbuf.at[pl.ds(0, QROWS)], qbuf.at[pl.ds(r * QROWS, QROWS)], coset(r, 1)))
-        for r in range(1, 8)
+        for r in (6, 2, 5, 7, 1, 3, 4)
     ]
     low, high = pl.ds(0, KEYS), pl.ds(KEYS, KEYS)
+    half_a, half_b = pl.ds(0, KEYS // 2), pl.ds(KEYS // 2, KEYS // 2)
+    tail_a, tail_b = pl.ds(KEYS, KEYS // 2), pl.ds(KEYS + KEYS // 2, KEYS // 2)
     local[1].wait()
     local[2].wait()
-    k_core = [None] * 4
-    v_core = [None] * 4
-    k_y = go(remote(kbuf.at[0, low], kbuf.at[1, low], dev_ynear))
-    v_z = go(remote(vbuf.at[0, low], vbuf.at[2, low], dev_znear))
-    v_y = go(remote(vbuf.at[0, low], vbuf.at[1, low], dev_ynear))
-    k_z = go(remote(kbuf.at[0, low], kbuf.at[2, low], dev_znear))
-    k_core[0] = go(remote(kbuf.at[0, low], kbuf.at[0, high], dev_core))
-    v_core[0] = go(remote(vbuf.at[0, low], vbuf.at[0, high], dev_core))
+    k_a = go(remote(kbuf.at[0, half_a], kbuf.at[1, half_a], dev_left))
+    k_b = go(remote(kbuf.at[0, half_b], kbuf.at[1, half_b], dev_right))
+    v_z = go(remote(vbuf.at[0, low], vbuf.at[1, high], dev_znear))
+    k_core = go(remote(kbuf.at[0, low], kbuf.at[0, high], dev_core))
+    v_core = go(remote(vbuf.at[0, low], vbuf.at[0, high], dev_core))
+    v_a = go(remote(vbuf.at[0, half_a], vbuf.at[1, half_a], dev_left))
+    v_b = go(remote(vbuf.at[0, half_b], vbuf.at[1, half_b], dev_right))
+    k_z = go(remote(kbuf.at[0, low], kbuf.at[1, high], dev_znear))
+    meet(0)
 
     for copy in local[3:5]:
         copy.wait()
@@ -185,35 +190,44 @@
 
         lax.fori_loop(0, 8 * QROWS // TILE, tile, 0)
 
-    k_core[0].wait_recv()
-    v_core[0].wait_recv()
+    k_core.wait_recv()
+    v_core.wait_recv()
     for copy in q_copies:
         copy.wait_recv()
     stage(0)
-    k_y.wait_recv()
+    k_a.wait_recv()
+    k_b.wait_recv()
     k_d = go(remote(kbuf.at[1, low], kbuf.at[3, low], dev_znear))
     v_z.wait_recv()
-    v_d = go(remote(vbuf.at[2, low], vbuf.at[3, low], dev_ynear))
-    v_y.wait_recv()
-    k_core[1] = go(remote(kbuf.at[1, low], kbuf.at[1, high], dev_core))
-    v_core[1] = go(remote(vbuf.at[1, low], vbuf.at[1, high], dev_core))
+    v_da = go(remote(vbuf.at[1, tail_a], vbuf.at[3, half_a], dev_left))
+    v_db = go(remote(vbuf.at[1, tail_b], vbuf.at[3, half_b], dev_right))
+    k_core = go(remote(kbuf.at[1, low], kbuf.at[2, low], dev_core))
+    v_core = go(remote(vbuf.at[1, high], vbuf.at[2, high], dev_core))
+    pl.semaphore_wait(met.at[0], len(steps))
+    meet(1)
+    v_a.wait_recv()
+    v_b.wait_recv()
+    v_core_y = go(remote(vbuf.at[1, low], vbuf.at[2, low], dev_core))
     k_z.wait_recv()
-    k_core[2] = go(remote(kbuf.at[2, low], kbuf.at[2, high], dev_core))
-    v_core[2] = go(remote(vbuf.at[2, low], vbuf.at[2, high], dev_core))
-    k_core[1].wait_recv()
-    v_core[1].wait_recv()
+    k_core_z = go(remote(kbuf.at[1, high], kbuf.at[2, high], dev_core))
     stage(1)
-    k_core[2].wait_recv()
-    v_core[2].wait_recv()
+    pl.semaphore_wait(met.at[1], len(steps))
+    meet(2)
+    k_core.wait_recv()
+    v_core.wait_recv()
+    v_core_y.wait_recv()
+    k_core_z.wait_recv()
+    k_d.wait_recv()
+    k_core = go(remote(kbuf.at[3, low], kbuf.at[3, high], dev_core))
+    v_da.wait_recv()
+    v_db.wait_recv()
+    v_core = go(remote(vbuf.at[3, low], vbuf.at[3, high], dev_core))
     stage(2)
-    k_d.wait_recv()
-    k_core[3] = go(remote(kbuf.at[3, low], kbuf.at[3, high], dev_core))
-    v_d.wait_recv()
-    v_core[3] = go(remote(vbuf.at[3, low], vbuf.at[3, high], dev_core))
     local[5].wait()
     w_copy = go(remote(wbuf.at[0], wbuf.at[1], dev_core))
-    k_core[3].wait_recv()
-    v_core[3].wait_recv()
+    pl.semaphore_wait(met.at[2], len(steps))
+    k_core.wait_recv()
+    v_core.wait_recv()
 
     part_slots = [(next(slots), next(slots)) for _ in range(7)]
     first_slot = part_slots[0][0]
@@ -276,22 +290,33 @@
     land[own] = jnp.concatenate(by_head, axis=0).astype(BF16)
 
     z_copies = [None] + [go(remote(land.at[own], land.at[own], line(r))) for r in range(1, NZ)]
-    arrived = {}
-    for k in range(4):
-        for r in range(NZ):
-            zz = lax.rem(z + r, NZ)
-            if k == 0 and r > 0:
-                z_copies[r].wait_recv()
-            for way in range(2):
-                if k > 0:
-                    arrived[way, k - 1, r].wait_recv()
-                if k == 3 and (r < 2) != (way == 0):
-                    continue
-                yy = lax.rem(y + NY - k, NY) if way == 0 else lax.rem(y + k, NY)
-                block = land.at[zz * NY + yy]
-                arrived[way, k, r] = go(remote(block, block, dev_right if way == 0 else dev_left))
+    ways = ((dev_right, coset(1, 1)), (dev_left, coset(1, -1)))
+    near, mid, far = {}, {}, {}
+
+    def block(r, dy):
+        return land.at[lax.rem(z + r, NZ) * NY + lax.rem(y + NY + dy, NY)]
+
+    def pass_on(r, way, dy, to):
+        return go(remote(block(r, dy), block(r, dy), to))
+
     for r in range(NZ):
-        arrived[0 if r < 2 else 1, 3, r].wait_recv()
+        if r > 0:
+            z_copies[r].wait_recv()
+        for way in range(2):
+            near[r, way] = pass_on(r, way, 0, ways[way][0])
+    for r in range(NZ):
+        for way in range(2):
+            near[r, way].wait_recv()
+            mid[r, way] = pass_on(r, way, (-1, 1)[way], ways[way][0])
+    for r in range(NZ):
+        for way in range(2):
+            mid[r, way].wait_recv()
+            far[r, way] = [pass_on(r, way, (-2, 2)[way], ways[way][0])]
+            if (r < 2) == (way == 0):
+                far[r, way].append(pass_on(r, way, (-2, 2)[way], ways[way][1]))
+    for copies in far.values():
+        for copy in copies:
+            copy.wait_recv()
 
     w_copy.wait_recv()
     for j in range(8):
@@ -326,7 +351,7 @@
     vmem = pltpu.VMEM
     return pl.pallas_call(
         kernel,
-        out_shape=jax.ShapeDtypeStruct((64, 256), BF16),
+        out_shape=pltpu.VMEM((64, 256), BF16),
         in_specs=[hbm] * 6 + [pl.BlockSpec(memory_space=vmem)] * 2 + [pl.BlockSpec(memory_space=pltpu.SMEM)],
         out_specs=pl.BlockSpec(memory_space=vmem),
         scratch_shapes=[
@@ -353,9 +378,10 @@
             pltpu.SemaphoreType.DMA((6,)),
             pltpu.SemaphoreType.DMA((96,)),
             pltpu.SemaphoreType.DMA((96,)),
+            pltpu.SemaphoreType.REGULAR((3,)),
         ],
         compiler_params=pltpu.CompilerParams(
-            collective_id=0, has_side_effects=True, vmem_limit_bytes=48 << 20
+            collective_id=0, has_side_effects=True, vmem_limit_bytes=60 << 20
         ),
         name="attend_project",
     )(

time: 84.6 us -> 73.6 us (0.87)
  local copies, waits for them, and re-layouts: 7.18 us -> 0.62 us
  Pallas kernels: 77 us -> 72.8 us
    unnamed x19 -> x1, local copies, waits for them, and re-layouts: 7.18 us -> 0.62 us
    pallas_call x1, Pallas kernels: 77 us -> 72.8 us  [on_device(): pl.pallas_call(kernel, out_shape=pltpu.VMEM((64, 256), BF16), in_specs=[h...]
where the time goes in v2:
time: 73.6 us; the launch traced here: 73.5 us
  Pallas kernels  72.8 us (99%)
    pallas_call x1, Pallas kernels, on_device(): pl.pallas_call(kernel, out_shape=pltpu.VMEM((64, 256), BF16), in_specs=[h...  72.8 us

profile of v2, /device:TPU:1, one launch (start us, length us, event | category | flops | bytes accessed | tf_op | source)
XLA Modules:
  0.0 73.5 jit_solution(1011705410811666026)
XLA Ops:
  0.0 72.8 %attend_project.1 = bf16[64,256]{1,0:T(8,128)(2,1)S(1)} custom-call(bf16[128,128]{1,0:T(8,128)(2,1)} %bitcast.11, bf16[512,128]{1,0:T(8,128)(2,1)} %bitcast.9, bf16[512,128]{1,0:T(8,128)(2,1)} %bitcast.10, bf16[8,256,128]{2,1,0:T(8,128)(2,1)} %bitcast.7, bf16[8,256,128]{2,1,0:T(8,128)(2,1)} %bitcast.8, bf16[2048,256]{1,0:T(8,128)(2,1)} %w_hbm.1, ...), custom_call_target="tpu_custom_call" | custom-call | tf_op jit(solution)/shard_map/attend_project/pallas_call | solution.py:352
  72.8 0.6 copy.11

commit v3 on v2

--- a/solution.py
+++ b/solution.py
@@ -33,13 +33,14 @@
     q_hbm, pk_hbm, pv_hbm, sk_hbm, sv_hbm, w_hbm, selfk_ref, selfv_ref, len_ref,
     out_ref,
     qbuf, kbuf, vbuf, skbuf, svbuf, selfk, selfv, wbuf,
-    num, top, den, pn_out, ps_out, pn_in, ps_in, att, land, rows_all, prod, pieces,
+    num, top, den, pn_out, ps_out, pn_in, ps_in, att, land, rows_all, prod, pieces, scores_a, scores_b,
     local_sem, send_sem, recv_sem, met,
 ):
     z, y, c, zh, x = coordinates()
     z_near = z + 1 - 2 * lax.rem(z, 2)
     other = 1 - c
     scale = math.log2(math.e) / math.sqrt(128)
+    scores = (scores_a, scores_b)
 
     local = [
         pltpu.make_async_copy(src, dst, local_sem.at[i])
@@ -69,8 +70,11 @@
             yy = lax.rem(y + NY - 2 * lax.rem(r, 4), NY)
         return device(zz, yy, c, zh, x)
 
-    def line(r):
-        return device(lax.rem(z + NZ - r, NZ), y, c, zh, x)
+    def z_other(m):
+        return (z, z_near, lax.rem(z + 2, NZ), NZ - 1 - z)[m]
+
+    def line(m):
+        return device(z_other(m), y, c, zh, x)
 
     dev_right = device(z, lax.rem(y + 1, NY), c, zh, x)
     dev_left = device(z, lax.rem(y + NY - 1, NY), c, zh, x)
@@ -110,18 +114,22 @@
             pl.semaphore_signal(met.at[i], inc=1, device_id=to, device_id_type=MESH)
 
     local[0].wait()
-    q_copies = [
-        go(remote(qbuf.at[pl.ds(0, QROWS)], qbuf.at[pl.ds(r * QROWS, QROWS)], coset(r, 1)))
-        for r in (6, 2, 5, 7, 1, 3, 4)
-    ]
     low, high = pl.ds(0, KEYS), pl.ds(KEYS, KEYS)
     half_a, half_b = pl.ds(0, KEYS // 2), pl.ds(KEYS // 2, KEYS // 2)
     tail_a, tail_b = pl.ds(KEYS, KEYS // 2), pl.ds(KEYS + KEYS // 2, KEYS // 2)
     local[1].wait()
     local[2].wait()
+    q_copies = {
+        r: go(remote(qbuf.at[pl.ds(0, QROWS)], qbuf.at[pl.ds(r * QROWS, QROWS)], coset(r, 1)))
+        for r in (6, 2, 5, 7)
+    }
     k_a = go(remote(kbuf.at[0, half_a], kbuf.at[1, half_a], dev_left))
     k_b = go(remote(kbuf.at[0, half_b], kbuf.at[1, half_b], dev_right))
     v_z = go(remote(vbuf.at[0, low], vbuf.at[1, high], dev_znear))
+    q_copies.update({
+        r: go(remote(qbuf.at[pl.ds(0, QROWS)], qbuf.at[pl.ds(r * QROWS, QROWS)], coset(r, 1)))
+        for r in (4, 1, 3)
+    })
     k_core = go(remote(kbuf.at[0, low], kbuf.at[0, high], dev_core))
     v_core = go(remote(vbuf.at[0, low], vbuf.at[0, high], dev_core))
     v_a = go(remote(vbuf.at[0, half_a], vbuf.at[1, half_a], dev_left))
@@ -161,48 +169,82 @@
 
     lax.fori_loop(0, 8, one_row, 0)
 
-    def absorb(g, i):
-        rows = pl.ds(pl.multiple_of(i * TILE, TILE), TILE)
-        s = lax.dot_general(
-            qbuf[rows, :], kbuf[g], (((1,), (1,)), ((), ())), preferred_element_type=F32
-        ) * scale
+    def score(g, i, buf):
+        rows = pl.ds(i * TILE, TILE)
+        best = None
+        for j in range(0, 2 * KEYS, 256):
+            s = lax.dot_general(
+                qbuf[rows, :], kbuf[g, j : j + 256, :], (((1,), (1,)), ((), ())), preferred_element_type=F32
+            )
+            buf[:, j : j + 256] = s
+            s = jnp.maximum(s[:, :128], s[:, 128:])
+            best = s if best is None else jnp.maximum(best, s)
+        return jnp.max(best, axis=1, keepdims=True) * scale
+
+    def absorb(g, i, buf, best):
+        rows = pl.ds(i * TILE, TILE)
         old = top[rows, :]
-        new = jnp.maximum(old, jnp.max(s, axis=1, keepdims=True))
+        new = jnp.maximum(old, best)
         base = jnp.exp2(-new)
         rescale = jnp.exp2(old - new)
         size = den[rows, :] * rescale
-        weights = []
-        for j in range(2 * KEYS // 128):
-            shifted = jnp.exp2(s[:, j * 128 : (j + 1) * 128] - new) - base
-            weights.append(jnp.maximum(shifted, 0.0).astype(BF16))
-            size = size + jnp.abs(shifted)
-        weights = jnp.concatenate(weights, axis=1)
-        total = num[rows, :] * rescale + jnp.dot(weights, vbuf[g], preferred_element_type=F32)
-        return rows, new, size, total
-
-    def stage(g):
-        def tile(i, carry):
-            rows, new, size, total = absorb(g, i)
-            top[rows, :] = new
-            den[rows, :] = size
-            num[rows, :] = total
-            return carry
-
-        lax.fori_loop(0, 8 * QROWS // TILE, tile, 0)
+        total = num[rows, :] * rescale
+        for j in range(0, 2 * KEYS, 256):
+            weights = []
+            for k in range(j, j + 256, 128):
+                shifted = jnp.exp2(buf[:, k : k + 128] * scale - new) - base
+                weights.append(jnp.maximum(shifted, 0.0).astype(BF16))
+                size = size + jnp.abs(shifted)
+            weights = jnp.concatenate(weights, axis=1)
+            total = total + jnp.dot(weights, vbuf[g, j : j + 256, :], preferred_element_type=F32)
+        return new, size, total
+
+    def stage(g, tiles, before, after):
+        before(tiles[0])
+        best = score(g, tiles[0], scores[0])
+        for n, i in enumerate(tiles):
+            if n + 1 < len(tiles):
+                before(tiles[n + 1])
+                best_next = score(g, tiles[n + 1], scores[(n + 1) % 2])
+            after(i, *absorb(g, i, scores[n % 2], best))
+            best = best_next
+
+    def nothing(i):
+        pass
+
+    def keep(i, new, size, total):
+        rows = pl.ds(i * TILE, TILE)
+        top[rows, :] = new
+        den[rows, :] = size
+        num[rows, :] = total
+
+    def await_queries(i):
+        for r in (2 * i, 2 * i + 1):
+            if r > 0:
+                q_copies[r].wait_recv()
+
+    def pass_near():
+        k_a.wait_recv()
+        k_b.wait_recv()
+        k_d = go(remote(kbuf.at[1, low], kbuf.at[3, low], dev_znear))
+        v_z.wait_recv()
+        v_da = go(remote(vbuf.at[1, tail_a], vbuf.at[3, half_a], dev_left))
+        v_db = go(remote(vbuf.at[1, tail_b], vbuf.at[3, half_b], dev_right))
+        k_core_y = go(remote(kbuf.at[1, low], kbuf.at[2, low], dev_core))
+        v_core_z = go(remote(vbuf.at[1, high], vbuf.at[2, high], dev_core))
+        return k_d, v_da, v_db, k_core_y, v_core_z
+
+    passed = []
+
+    def before_first(i):
+        if i == 2:
+            passed.extend(pass_near())
+        await_queries(i)
 
     k_core.wait_recv()
     v_core.wait_recv()
-    for copy in q_copies:
-        copy.wait_recv()
-    stage(0)
-    k_a.wait_recv()
-    k_b.wait_recv()
-    k_d = go(remote(kbuf.at[1, low], kbuf.at[3, low], dev_znear))
-    v_z.wait_recv()
-    v_da = go(remote(vbuf.at[1, tail_a], vbuf.at[3, half_a], dev_left))
-    v_db = go(remote(vbuf.at[1, tail_b], vbuf.at[3, half_b], dev_right))
-    k_core = go(remote(kbuf.at[1, low], kbuf.at[2, low], dev_core))
-    v_core = go(remote(vbuf.at[1, high], vbuf.at[2, high], dev_core))
+    stage(0, (0, 1, 2, 3), before_first, keep)
+    k_d, v_da, v_db, k_core_y, v_core_z = passed
     pl.semaphore_wait(met.at[0], len(steps))
     meet(1)
     v_a.wait_recv()
@@ -210,11 +252,11 @@
     v_core_y = go(remote(vbuf.at[1, low], vbuf.at[2, low], dev_core))
     k_z.wait_recv()
     k_core_z = go(remote(kbuf.at[1, high], kbuf.at[2, high], dev_core))
-    stage(1)
+    stage(1, (0, 1, 2, 3), nothing, keep)
     pl.semaphore_wait(met.at[1], len(steps))
     meet(2)
-    k_core.wait_recv()
-    v_core.wait_recv()
+    k_core_y.wait_recv()
+    v_core_z.wait_recv()
     v_core_y.wait_recv()
     k_core_z.wait_recv()
     k_d.wait_recv()
@@ -222,7 +264,7 @@
     v_da.wait_recv()
     v_db.wait_recv()
     v_core = go(remote(vbuf.at[3, low], vbuf.at[3, high], dev_core))
-    stage(2)
+    stage(2, (0, 1, 2, 3), nothing, keep)
     local[5].wait()
     w_copy = go(remote(wbuf.at[0], wbuf.at[1], dev_core))
     pl.semaphore_wait(met.at[2], len(steps))
@@ -238,8 +280,8 @@
         return both.T[0:8, :]
 
     def part_copies(r):
-        rows = pl.ds(pl.multiple_of(r * QROWS, QROWS), QROWS)
-        stat = pl.ds(pl.multiple_of(r * 8, 8), 8)
+        rows = pl.ds(r * QROWS, QROWS)
+        stat = pl.ds(r * 8, 8)
         to = coset(r, -1)
         slot = first_slot + 2 * (r - 1)
         return (
@@ -247,28 +289,19 @@
             remote(ps_out.at[stat], ps_in.at[stat], to, slot + 1),
         )
 
-    def last(i):
-        rows, new, size, total = absorb(3, i)
-        pn_out[rows, :] = total.astype(BF16)
+    def send_parts(i, new, size, total):
+        pn_out[pl.ds(i * TILE, TILE), :] = total.astype(BF16)
         for half in range(2):
             part = slice(half * QROWS, (half + 1) * QROWS)
             r = i * 2 + half
-            ps_out[pl.ds(pl.multiple_of(r * 8, 8), 8), :] = stat_rows(new[part], size[part])
-        return total
-
-    def last_tile(step, carry):
-        i = 3 - step
-        last(i)
-        for half in range(2):
-            for copy in part_copies(i * 2 + half):
-                copy.start()
-        return carry
-
-    lax.fori_loop(0, 3, last_tile, 0)
-    total = last(0)
-    for copy in part_copies(1):
-        copy.start()
-    num[pl.ds(0, QROWS), :] = total[:QROWS]
+            ps_out[pl.ds(r * 8, 8), :] = stat_rows(new[part], size[part])
+            if r > 0:
+                for copy in part_copies(r):
+                    copy.start()
+        if i == 0:
+            num[pl.ds(0, QROWS), :] = total[:QROWS]
+
+    stage(3, (3, 2, 1, 0), nothing, send_parts)
 
     for r in range(1, 8):
         for copy in part_copies(r):
@@ -289,53 +322,86 @@
     own = z * NY + y
     land[own] = jnp.concatenate(by_head, axis=0).astype(BF16)
 
-    z_copies = [None] + [go(remote(land.at[own], land.at[own], line(r))) for r in range(1, NZ)]
+    z_first = [next(slots) for _ in range(NZ)][0]
+
+    def z_copy(m):
+        return remote(land.at[own], land.at[own], line(m), z_first + m)
+
+    for m in range(1, NZ):
+        go(z_copy(m))
     ways = ((dev_right, coset(1, 1)), (dev_left, coset(1, -1)))
     near, mid, far = {}, {}, {}
+    same = 1 - (z // 2 + zh - 2 * (z // 2) * zh)
+    z_order = [
+        z,
+        same * z_other(2) + (1 - same) * z_other(1),
+        same * z_other(3) + (1 - same) * z_other(2),
+        same * z_other(1) + (1 - same) * z_other(3),
+    ]
+    bits = [0, 1 + same, 2 + same, 3 - 2 * same]
 
     def block(r, dy):
-        return land.at[lax.rem(z + r, NZ) * NY + lax.rem(y + NY + dy, NY)]
+        return land.at[z_order[r] * NY + lax.rem(y + NY + dy, NY)]
 
     def pass_on(r, way, dy, to):
         return go(remote(block(r, dy), block(r, dy), to))
 
-    for r in range(NZ):
+    def send_near(r):
         if r > 0:
-            z_copies[r].wait_recv()
+            remote(land.at[own], land.at[own], dev_znear, z_first + bits[r]).wait_recv()
         for way in range(2):
             near[r, way] = pass_on(r, way, 0, ways[way][0])
-    for r in range(NZ):
+
+    def send_mid(r):
         for way in range(2):
             near[r, way].wait_recv()
             mid[r, way] = pass_on(r, way, (-1, 1)[way], ways[way][0])
-    for r in range(NZ):
+
+    def send_far(r):
         for way in range(2):
             mid[r, way].wait_recv()
             far[r, way] = [pass_on(r, way, (-2, 2)[way], ways[way][0])]
             if (r < 2) == (way == 0):
                 far[r, way].append(pass_on(r, way, (-2, 2)[way], ways[way][1]))
-    for copies in far.values():
-        for copy in copies:
-            copy.wait_recv()
-
-    w_copy.wait_recv()
-    for j in range(8):
-        pair = land[:, j * 16 : (j + 1) * 16, :].astype(F32).reshape(32, 2, 8, 128)
-        for half in range(2):
-            h = 2 * j + half
-            rows_all[:, h * 128 : (h + 1) * 128] = pair[:, half].reshape(256, 128).astype(BF16)
-    prod[0] = jnp.dot(rows_all[...], wbuf[0], preferred_element_type=F32).astype(BF16)
-    prod[1] = jnp.dot(rows_all[...], wbuf[1], preferred_element_type=F32).astype(BF16)
+
+    for step in (send_near, send_mid, send_far):
+        for r in range(NZ):
+            step(r)
+    def finish_gather(r):
+        for way in range(2):
+            for copy in far[r, way]:
+                copy.wait_recv()
+
+    def project(side):
+        first = pl.multiple_of(side * 16, 16)
+        for j in range(8):
+            pair = land[pl.ds(first, 16), j * 16 : (j + 1) * 16, :].astype(F32).reshape(16, 2, 8, 128)
+            for half in range(2):
+                h = 2 * j + half
+                rows_all[:, h * 128 : (h + 1) * 128] = pair[:, half].reshape(128, 128).astype(BF16)
+        rows = pl.ds(pl.multiple_of(side * 128, 128), 128)
+        for core in range(2):
+            prod[core, rows, :] = jnp.dot(rows_all[...], wbuf[core], preferred_element_type=F32).astype(BF16)
 
     def piece(r):
         t = lax.rem(zh + r // 8, NZH) * NX + lax.rem(x + lax.rem(r // 2, 4), NX)
         return prod.at[r % 2, pl.ds(pl.multiple_of(t * 32, 32), 32)]
 
-    out_copies = [go(remote(piece(r), pieces.at[r], owner(r))) for r in range(1, 16)]
+    def send_piece(r):
+        return go(remote(piece(r), pieces.at[r], owner(r)))
+
+    for r in range(3):
+        finish_gather(r)
+    w_copy.wait_recv()
+    project(1 - zh)
+    out_copies = {r: send_piece(r) for r in (12, 13, 10, 11, 14, 15, 8, 9)}
+    finish_gather(3)
+    project(zh)
+    out_copies.update({r: send_piece(r) for r in (4, 5, 2, 3, 6, 7, 1)})
     own_rows = pl.ds(pl.multiple_of((zh * NX + x) * 32, 32), 32)
     sums = [prod[0, own_rows, :].astype(F32), None]
     for r in range(1, 16):
-        out_copies[r - 1].wait_recv()
+        out_copies[r].wait_recv()
         term = pieces[r].astype(F32)
         sums[r % 2] = term if sums[r % 2] is None else sums[r % 2] + term
     first = jnp.where(c == 0, sums[0], sums[1]).reshape(4, 1, 8, 256)
@@ -372,9 +438,11 @@
             vmem((64, 128), F32),
             vmem((QROWS, 128), F32),
             vmem((32, QROWS, 128), BF16),
-            vmem((256, 2048), BF16),
+            vmem((128, 2048), BF16),
             vmem((2, 256, 256), BF16),
             vmem((16, 32, 256), BF16),
+            vmem((TILE, 2 * KEYS), F32),
+            vmem((TILE, 2 * KEYS), F32),
             pltpu.SemaphoreType.DMA((6,)),
             pltpu.SemaphoreType.DMA((96,)),
             pltpu.SemaphoreType.DMA((96,)),

time: 73.6 us -> 69.2 us (0.940)
  Pallas kernels: 72.8 us -> 68.5 us
    pallas_call x1, Pallas kernels: 72.8 us -> 68.5 us  [on_device(): pl.pallas_call(kernel, out_shape=pltpu.VMEM((64, 256), BF16), in_specs=[h...]
where the time goes in v3:
time: 69.2 us; the launch traced here: 69.1 us
  Pallas kernels  68.5 us (99%)
    pallas_call x1, Pallas kernels, on_device(): pl.pallas_call(kernel, out_shape=pltpu.VMEM((64, 256), BF16), in_specs=[h...  68.5 us

profile of v3, /device:TPU:1, one launch (start us, length us, event | category | flops | bytes accessed | tf_op | source)
XLA Modules:
  0.0 69.1 jit_solution(15947599343680900045)
XLA Ops:
  0.0 68.5 %attend_project.1 = bf16[64,256]{1,0:T(8,128)(2,1)S(1)} custom-call(bf16[128,128]{1,0:T(8,128)(2,1)} %bitcast.11, bf16[512,128]{1,0:T(8,128)(2,1)} %bitcast.9, bf16[512,128]{1,0:T(8,128)(2,1)} %bitcast.10, bf16[8,256,128]{2,1,0:T(8,128)(2,1)} %bitcast.7, bf16[8,256,128]{2,1,0:T(8,128)(2,1)} %bitcast.8, bf16[2048,256]{1,0:T(8,128)(2,1)} %w_hbm.1, ...), custom_call_target="tpu_custom_call" | custom-call | tf_op jit(solution)/shard_map/attend_project/pallas_call | solution.py:418
  68.5 0.6 copy.11

commit v4 on v3

--- a/solution.py
+++ b/solution.py
@@ -76,6 +76,9 @@
     def line(m):
         return device(z_other(m), y, c, zh, x)
 
+    def along_y(d):
+        return device(z, lax.rem(y + d, NY), c, zh, x)
+
     dev_right = device(z, lax.rem(y + 1, NY), c, zh, x)
     dev_left = device(z, lax.rem(y + NY - 1, NY), c, zh, x)
 
@@ -88,6 +91,7 @@
     partners = [dev_right, dev_left] + steps
     partners += [coset(r, 1) for r in range(1, 8)]
     partners += [line(r) for r in range(1, NZ)]
+    partners += [along_y(3), along_y(5)]
     barrier = pltpu.get_barrier_semaphore()
     for partner in partners:
         pl.semaphore_signal(barrier, inc=1, device_id=partner, device_id_type=MESH)
@@ -145,29 +149,38 @@
     top[...] = jnp.zeros_like(top)
     den[...] = jnp.zeros_like(den)
 
-    def one_row(r, carry):
-        rows = pl.ds(pl.multiple_of(r * 16, 16), 16)
-        q = qbuf[rows, :]
-        s = lax.dot_general(q, skbuf[r], (((1,), (1,)), ((), ())), preferred_element_type=F32) * scale
-        live = lax.broadcasted_iota(jnp.int32, s.shape, 1) < len_ref[r]
-        s = jnp.where(live, s, 0.0)
-        s_self = jnp.sum(q.astype(F32) * selfk[pl.ds(r, 1), :], axis=1, keepdims=True) * scale
-        m = jnp.maximum(jnp.maximum(jnp.max(s, axis=1, keepdims=True), s_self), 0.0)
-        base = jnp.exp2(-m)
-        shifted = jnp.where(live, jnp.exp2(s - m) - base, 0.0)
-        shifted_self = jnp.exp2(s_self - m) - base
-        weights = jnp.maximum(shifted, 0.0).astype(BF16)
-        weight_self = jnp.maximum(shifted_self, 0.0).astype(BF16).astype(F32)
-        total = jnp.dot(weights, svbuf[r], preferred_element_type=F32)
-        num[rows, :] = total + weight_self * selfv[pl.ds(r, 1), :]
-        size = jnp.abs(shifted)
-        size = size[:, :128] + size[:, 128:]
-        lane = lax.broadcasted_iota(jnp.int32, size.shape, 1)
-        den[rows, :] = size + jnp.where(lane == 0, jnp.abs(shifted_self), 0.0)
-        top[rows, :] = jnp.broadcast_to(m, size.shape)
-        return carry
-
-    lax.fori_loop(0, 8, one_row, 0)
+    own_rows = pl.ds(0, QROWS)
+    q = qbuf[own_rows, :]
+    by_row = [slice(r * 16, (r + 1) * 16) for r in range(8)]
+
+    def spread(values):
+        return jnp.concatenate(values, axis=0)
+
+    s = spread([
+        lax.dot_general(q[part], skbuf[r], (((1,), (1,)), ((), ())), preferred_element_type=F32)
+        for r, part in enumerate(by_row)
+    ]) * scale
+    lengths = spread([jnp.full((16, s.shape[1]), len_ref[r], jnp.int32) for r in range(8)])
+    live = lax.broadcasted_iota(jnp.int32, s.shape, 1) < lengths
+    s = jnp.where(live, s, 0.0)
+    own_keys = spread([jnp.broadcast_to(selfk[r : r + 1, :], (16, 128)) for r in range(8)])
+    own_values = spread([jnp.broadcast_to(selfv[r : r + 1, :], (16, 128)) for r in range(8)])
+    s_self = jnp.sum(q.astype(F32) * own_keys, axis=1, keepdims=True) * scale
+    m = jnp.maximum(jnp.maximum(jnp.max(s, axis=1, keepdims=True), s_self), 0.0)
+    base = jnp.exp2(-m)
+    shifted = jnp.where(live, jnp.exp2(s - m) - base, 0.0)
+    shifted_self = jnp.exp2(s_self - m) - base
+    weights = jnp.maximum(shifted, 0.0).astype(BF16)
+    weight_self = jnp.maximum(shifted_self, 0.0).astype(BF16).astype(F32)
+    total = spread([
+        jnp.dot(weights[part], svbuf[r], preferred_element_type=F32) for r, part in enumerate(by_row)
+    ])
+    num[own_rows, :] = total + weight_self * own_values
+    size = jnp.abs(shifted)
+    size = size[:, :128] + size[:, 128:]
+    lane = lax.broadcasted_iota(jnp.int32, size.shape, 1)
+    den[own_rows, :] = size + jnp.where(lane == 0, jnp.abs(shifted_self), 0.0)
+    top[own_rows, :] = jnp.broadcast_to(m, size.shape)
 
     def score(g, i, buf):
         rows = pl.ds(i * TILE, TILE)
@@ -322,10 +335,16 @@
     own = z * NY + y
     land[own] = jnp.concatenate(by_head, axis=0).astype(BF16)
 
+    heads_y, heads_z = pl.ds(0, 32), pl.ds(32, 96)
     z_first = [next(slots) for _ in range(NZ)][0]
+    line_first = [next(slots) for _ in range(NZ)][0]
 
     def z_copy(m):
-        return remote(land.at[own], land.at[own], line(m), z_first + m)
+        return remote(land.at[own, heads_z], land.at[own, heads_z], line(m), z_first + m)
+
+    def line_copy(m):
+        whole = land.at[pl.ds(pl.multiple_of(z * NY, NY), NY), heads_y]
+        return remote(whole, whole, line(m), line_first + m)
 
     for m in range(1, NZ):
         go(z_copy(m))
@@ -341,14 +360,14 @@
     bits = [0, 1 + same, 2 + same, 3 - 2 * same]
 
     def block(r, dy):
-        return land.at[z_order[r] * NY + lax.rem(y + NY + dy, NY)]
+        return land.at[z_order[r] * NY + lax.rem(y + NY + dy, NY), heads_z]
 
     def pass_on(r, way, dy, to):
         return go(remote(block(r, dy), block(r, dy), to))
 
     def send_near(r):
         if r > 0:
-            remote(land.at[own], land.at[own], dev_znear, z_first + bits[r]).wait_recv()
+            remote(land.at[own, heads_z], land.at[own, heads_z], dev_znear, z_first + bits[r]).wait_recv()
         for way in range(2):
             near[r, way] = pass_on(r, way, 0, ways[way][0])
 
@@ -364,10 +383,26 @@
             if (r < 2) == (way == 0):
                 far[r, way].append(pass_on(r, way, (-2, 2)[way], ways[way][1]))
 
-    for step in (send_near, send_mid, send_far):
-        for r in range(NZ):
-            step(r)
+    send_near(0)
+    y_copies = [
+        go(remote(land.at[own, heads_y], land.at[own, heads_y], along_y(d))) for d in (4, 3, 5, 2, 6, 1, 7)
+    ]
+    for r in range(1, NZ):
+        send_near(r)
+    send_mid(0)
+    for copy in y_copies:
+        copy.wait_recv()
+    for m in range(1, NZ):
+        go(line_copy(m))
+    for r in range(1, NZ):
+        send_mid(r)
+    for r in range(NZ):
+        send_far(r)
+
     def finish_gather(r):
+        if r > 0:
+            whole = land.at[pl.ds(pl.multiple_of(z * NY, NY), NY), heads_y]
+            remote(whole, whole, dev_znear, line_first + bits[r]).wait_recv()
         for way in range(2):
             for copy in far[r, way]:
                 copy.wait_recv()
@@ -444,8 +479,8 @@
             vmem((TILE, 2 * KEYS), F32),
             vmem((TILE, 2 * KEYS), F32),
             pltpu.SemaphoreType.DMA((6,)),
-            pltpu.SemaphoreType.DMA((96,)),
-            pltpu.SemaphoreType.DMA((96,)),
+            pltpu.SemaphoreType.DMA((128,)),
+            pltpu.SemaphoreType.DMA((128,)),
             pltpu.SemaphoreType.REGULAR((3,)),
         ],
         compiler_params=pltpu.CompilerParams(

time: 69.2 us -> 68.9 us (level)
  no operation moved by 1% of the time
where the time goes in v4:
time: 68.9 us; the launch traced here: 68.7 us
  Pallas kernels  68.1 us (99%)
    pallas_call x1, Pallas kernels, on_device(): pl.pallas_call(kernel, out_shape=pltpu.VMEM((64, 256), BF16), in_specs=[h...  68.1 us

profile of v4, /device:TPU:1, one launch (start us, length us, event | category | flops | bytes accessed | tf_op | source)
XLA Modules:
  0.0 68.7 jit_solution(8094819786310578779)
XLA Ops:
  0.0 68.1 %attend_project.1 = bf16[64,256]{1,0:T(8,128)(2,1)S(1)} custom-call(bf16[128,128]{1,0:T(8,128)(2,1)} %bitcast.11, bf16[512,128]{1,0:T(8,128)(2,1)} %bitcast.9, bf16[512,128]{1,0:T(8,128)(2,1)} %bitcast.10, bf16[8,256,128]{2,1,0:T(8,128)(2,1)} %bitcast.7, bf16[8,256,128]{2,1,0:T(8,128)(2,1)} %bitcast.8, bf16[2048,256]{1,0:T(8,128)(2,1)} %w_hbm.1, ...), custom_call_target="tpu_custom_call" | custom-call | tf_op jit(solution)/shard_map/attend_project/pallas_call | solution.py:453
  68.1 0.6 copy.11

commit v5 on v4

--- a/solution.py
+++ b/solution.py
@@ -250,7 +250,7 @@
     passed = []
 
     def before_first(i):
-        if i == 2:
+        if i == 0:
             passed.extend(pass_near())
         await_queries(i)
 

time: 68.9 us -> 68.8 us (level)
  no operation moved by 1% of the time
where the time goes in v5:
time: 68.8 us; the launch traced here: 68.6 us
  Pallas kernels  68 us (99%)
    pallas_call x1, Pallas kernels, on_device(): pl.pallas_call(kernel, out_shape=pltpu.VMEM((64, 256), BF16), in_specs=[h...  68 us

profile of v5, /device:TPU:1, one launch (start us, length us, event | category | flops | bytes accessed | tf_op | source)
XLA Modules:
  0.0 68.6 jit_solution(5870994250063062289)
XLA Ops:
  0.0 68.0 %attend_project.1 = bf16[64,256]{1,0:T(8,128)(2,1)S(1)} custom-call(bf16[128,128]{1,0:T(8,128)(2,1)} %bitcast.11, bf16[512,128]{1,0:T(8,128)(2,1)} %bitcast.9, bf16[512,128]{1,0:T(8,128)(2,1)} %bitcast.10, bf16[8,256,128]{2,1,0:T(8,128)(2,1)} %bitcast.7, bf16[8,256,128]{2,1,0:T(8,128)(2,1)} %bitcast.8, bf16[2048,256]{1,0:T(8,128)(2,1)} %w_hbm.1, ...), custom_call_target="tpu_custom_call" | custom-call | tf_op jit(solution)/shard_map/attend_project/pallas_call | solution.py:453
  68.0 0.6 copy.11
